TPU v7x, 32 devices: a whole 2x2x4 slice. The times are simulated.
32 devices in a mesh: ctx: 4 (over z), head: 8 (over y, x, core).
Axes of the slice: x: 2, y: 2, z: 4, core: 2. Of those that a mesh axis runs over, the one named last changes fastest.
Arguments:
- queries: bfloat16 [4096, 24576], P('ctx', 'head'), may hold values from -110 to 110
- latent_kv: bfloat16 [4096, 576], P('ctx'), may hold values from -6 to 6
- w_uk: bfloat16 [128, 512, 128], P('head'), may hold values from -0.25 to 0.25
- w_uv: bfloat16 [128, 512, 128], P('head'), may hold values from -0.25 to 0.25
- grad_out: bfloat16 [4096, 16384], P('ctx', 'head'), may hold values from -48 to 48
Outputs:
- grad_queries: bfloat16 [4096, 24576], P('ctx', 'head')
- grad_latent: float32 [4096, 576], P(('ctx', 'head'))
All inputs are finite; a program needn't handle non-finite values.
Results may differ from a plain program's by a relative error of at most 0.013.
Values may be sent and summed in bfloat16 or wider, within the bound.
A program may use at most 192 MiB of HBM per device.

v0:
```python
import jax
import jax.numpy as jnp
from jax import lax
from jax.sharding import PartitionSpec as P

W = 512
TILE = 128


def from_behind(array, axis, by):
    peers = lax.axis_size(axis)
    pairs = [(i, i + by) for i in range(peers) if 0 <= i + by < peers]
    return lax.ppermute(array, axis, pairs)


def project_keys(latent_rows, w_uk, w_uv):
    latent_part = latent_rows[:, : w_uk.shape[1]]
    keys_nope = jnp.einsum(
        "td,hdn->thn", latent_part, w_uk, preferred_element_type=jnp.float32
    ).astype(jnp.bfloat16)
    values = jnp.einsum(
        "td,hdv->thv", latent_part, w_uv, preferred_element_type=jnp.float32
    ).astype(jnp.bfloat16)
    return (keys_nope, values)


def project_back(key_gradient, value_gradient, rotary_gradient, key_weight, value_weight):
    latent_grad = jnp.einsum(
        "thn,hdn->td", key_gradient, key_weight, precision=lax.Precision.HIGHEST
    )
    latent_grad = latent_grad + jnp.einsum(
        "thv,hdv->td", value_gradient, value_weight, precision=lax.Precision.HIGHEST
    )
    return jnp.concatenate([latent_grad, rotary_gradient], axis=1)


def shards(queries, latent_kv, w_uk, w_uv, grad_out):
    token_count = queries.shape[0]
    heads_here = w_uk.shape[0]
    latent_dim = w_uk.shape[1]
    nope_dim = w_uk.shape[2]
    value_dim = w_uv.shape[2]
    row_dim = latent_kv.shape[1]
    rope_dim = row_dim - latent_dim
    query_dim = nope_dim + rope_dim
    window_len = W
    tile_rows = TILE
    span_rows = tile_rows + window_len
    score_scale = query_dim ** (-0.5)
    query_rows = queries.reshape(token_count, heads_here, query_dim)
    grad_rows = grad_out.reshape(token_count, heads_here, value_dim)
    edge_latent = latent_kv[token_count - window_len :]
    previous = from_behind(edge_latent, "ctx", 1)
    extended = jnp.concatenate([previous, latent_kv], axis=0)
    keys_ext, values_ext = project_keys(extended, w_uk, w_uv)
    rope_ext = extended[:, latent_dim:]
    is_first = lax.axis_index("ctx") == 0
    lower_idx = jnp.arange(tile_rows)[:, None]
    upper_idx = jnp.arange(span_rows)[None, :]
    band = (upper_idx > lower_idx) & (upper_idx <= lower_idx + window_len)

    def tile_advance(carry, block):
        acc_keys, acc_values, acc_rope = carry
        first_row = block * tile_rows
        q_block = lax.dynamic_slice_in_dim(query_rows, first_row, tile_rows, 0)
        g_block = lax.dynamic_slice_in_dim(grad_rows, first_row, tile_rows, 0)
        k_block = lax.dynamic_slice_in_dim(keys_ext, first_row, span_rows, 0)
        v_block = lax.dynamic_slice_in_dim(values_ext, first_row, span_rows, 0)
        r_block = lax.dynamic_slice_in_dim(rope_ext, first_row, span_rows, 0)
        query_unrotated = q_block[:, :, :nope_dim]
        query_rotary = q_block[:, :, nope_dim:]
        logit_scores = jnp.einsum(
            "qhn,khn->hqk", query_unrotated, k_block, preferred_element_type=jnp.float32
        )
        logit_scores = logit_scores + jnp.einsum(
            "qhr,kr->hqk", query_rotary, r_block, preferred_element_type=jnp.float32
        )
        allowed = band & jnp.logical_not(is_first & (first_row + upper_idx < window_len))
        logit_scores = jnp.where(allowed[None], logit_scores * score_scale, -jnp.inf)
        peak = jnp.max(logit_scores, axis=2, keepdims=True)
        expo = jnp.exp(logit_scores - peak)
        probs = expo / jnp.sum(expo, axis=2, keepdims=True)
        lowered_probabilities = probs.astype(jnp.bfloat16)
        attended_output = jnp.einsum(
            "hqk,khv->qhv", lowered_probabilities, v_block, preferred_element_type=jnp.float32
        )
        delta = jnp.transpose(jnp.sum(g_block.astype(jnp.float32) * attended_output, axis=2))
        probability_gradient = jnp.einsum(
            "qhv,khv->hqk", g_block, v_block, preferred_element_type=jnp.float32
        )
        similarity_derivative = (probs * (probability_gradient - delta[:, :, None])).astype(
            jnp.bfloat16
        )
        unrotated_gradient = jnp.einsum(
            "hqk,khn->qhn", similarity_derivative, k_block, preferred_element_type=jnp.float32
        )
        positional_request_derivative = jnp.einsum(
            "hqk,kr->qhr", similarity_derivative, r_block, preferred_element_type=jnp.float32
        )
        grad_query = (
            jnp.concatenate([unrotated_gradient, positional_request_derivative], axis=2)
            * score_scale
        ).astype(jnp.bfloat16)
        new_keys = (
            jnp.einsum(
                "hqk,qhn->khn",
                similarity_derivative,
                query_unrotated,
                preferred_element_type=jnp.float32,
            )
            * score_scale
        )
        new_values = jnp.einsum(
            "hqk,qhv->khv", lowered_probabilities, g_block, preferred_element_type=jnp.float32
        )
        new_rope = (
            jnp.einsum(
                "hqk,qhr->kr",
                similarity_derivative,
                query_rotary,
                preferred_element_type=jnp.float32,
            )
            * score_scale
        )
        acc_keys = lax.dynamic_update_slice_in_dim(
            acc_keys,
            lax.dynamic_slice_in_dim(acc_keys, first_row, span_rows, 0) + new_keys,
            first_row,
            0,
        )
        acc_values = lax.dynamic_update_slice_in_dim(
            acc_values,
            lax.dynamic_slice_in_dim(acc_values, first_row, span_rows, 0) + new_values,
            first_row,
            0,
        )
        acc_rope = lax.dynamic_update_slice_in_dim(
            acc_rope,
            lax.dynamic_slice_in_dim(acc_rope, first_row, span_rows, 0) + new_rope,
            first_row,
            0,
        )
        return ((acc_keys, acc_values, acc_rope), grad_query)

    ext_rows = token_count + window_len
    initial_state = (
        jnp.zeros((ext_rows, heads_here, nope_dim), jnp.float32),
        jnp.zeros((ext_rows, heads_here, value_dim), jnp.float32),
        jnp.zeros((ext_rows, rope_dim), jnp.float32),
    )
    block_ids = jnp.arange(token_count // tile_rows, dtype=jnp.int32)
    final_carry, grad_blocks = lax.scan(tile_advance, initial_state, block_ids)
    acc_keys, acc_values, acc_rope = final_carry
    grad_queries = grad_blocks.reshape(token_count, heads_here * query_dim)
    key_weight = w_uk.astype(jnp.float32)
    value_weight = w_uv.astype(jnp.float32)
    edge_grad = project_back(
        acc_keys[:window_len],
        acc_values[:window_len],
        acc_rope[:window_len],
        key_weight,
        value_weight,
    )
    returned = from_behind(edge_grad.astype(jnp.bfloat16), "ctx", -1).astype(edge_grad.dtype)
    extra_rows = jnp.concatenate(
        [jnp.zeros((token_count - window_len, row_dim), jnp.float32), returned], axis=0
    )
    own_keys = acc_keys[window_len:]
    own_values = acc_values[window_len:]
    own_rope = acc_rope[window_len:]
    row_share = token_count // lax.axis_size("head")
    added_together = lax.psum(
        project_back(own_keys, own_values, own_rope, key_weight, value_weight) + extra_rows, "head"
    )
    grad_latent = lax.dynamic_slice_in_dim(
        added_together, lax.axis_index("head") * row_share, row_share, 0
    )
    return (grad_queries, grad_latent)


def solution(mesh):
    in_specs = (
        P("ctx", "head"),
        P("ctx", None),
        P("head", None, None),
        P("head", None, None),
        P("ctx", "head"),
    )
    out_specs = (P("ctx", "head"), P(("ctx", "head"), None))
    return jax.shard_map(shards, mesh=mesh, in_specs=in_specs, out_specs=out_specs, check_vma=False)
```

profile of v0, /device:TPU:0, one launch (start us, length us, event | category | flops | bytes accessed | tf_op | source)
XLA Modules:
  0.0 971.6 jit_solution(16143185035174829457)
XLA Ops:
  23.6 8.5 copy.52
  62.5 797.1 %while.17 = (s32[]{:T(128)}, f32[1536,16,128]{2,0,1:T(8,128)}, f32[1536,16,128]{2,0,1:T(8,128)}, f32[1536,64]{0,1:T(8,128)}, bf16[8,128,16,192]{1,3,2,0:T(8,128)...) while((s32[]{:T(128)}, f32[1536,16,128]{2,0,1:T(8,128)}, ...), condition=%wide.region_4.5_spmd.clone, body=%wide.region_0.4_spmd.clone.sunk | while | flops 2542557696 | bytes 264161616 | solution.py:152
  106.6 7.2 fusion.149
  113.8 9.0 fusion.150
  122.8 12.0 %bitcast_add_fusion.6 = f32[640,16,128]{0,2,1:T(8,128)} fusion(f32[640,16,128]{0,2,1:T(8,128)} %copy.90, bf16[128,16,128]{0,2,1:T(8,128)(2,1)S(1)} %constant_dynamic-slice_fusion.8, f32[16,128]{1,0:T(8,128)S(1)} %get-tuple-element.267, f32[16,128,640]{2,1,0:T(8,128)} %fusion.148), kind=kOutput, calls=%fused_computation.3.clone.1 | convolution fusion | flops 340789888 | bytes 16261120 | tf_op jit(solution)/shard_map/while/body/eval_jaxpr/hqk,qhv->khv/dot_general | solution.py:113
  212.0 9.1 fusion.150
  221.1 12.0 %bitcast_add_fusion.6 = f32[640,16,128]{0,2,1:T(8,128)} fusion(f32[640,16,128]{0,2,1:T(8,128)} %copy.90, bf16[128,16,128]{0,2,1:T(8,128)(2,1)S(1)} %constant_dynamic-slice_fusion.8, f32[16,128]{1,0:T(8,128)S(1)} %get-tuple-element.267, f32[16,128,640]{2,1,0:T(8,128)} %fusion.148), kind=kOutput, calls=%fused_computation.3.clone.1 | convolution fusion | flops 340789888 | bytes 16261120 | tf_op jit(solution)/shard_map/while/body/eval_jaxpr/hqk,qhv->khv/dot_general | solution.py:113
  310.2 9.0 fusion.150
  319.3 12.0 %bitcast_add_fusion.6 = f32[640,16,128]{0,2,1:T(8,128)} fusion(f32[640,16,128]{0,2,1:T(8,128)} %copy.90, bf16[128,16,128]{0,2,1:T(8,128)(2,1)S(1)} %constant_dynamic-slice_fusion.8, f32[16,128]{1,0:T(8,128)S(1)} %get-tuple-element.267, f32[16,128,640]{2,1,0:T(8,128)} %fusion.148), kind=kOutput, calls=%fused_computation.3.clone.1 | convolution fusion | flops 340789888 | bytes 16261120 | tf_op jit(solution)/shard_map/while/body/eval_jaxpr/hqk,qhv->khv/dot_general | solution.py:113
  408.6 9.0 fusion.150
  417.6 12.0 %bitcast_add_fusion.6 = f32[640,16,128]{0,2,1:T(8,128)} fusion(f32[640,16,128]{0,2,1:T(8,128)} %copy.90, bf16[128,16,128]{0,2,1:T(8,128)(2,1)S(1)} %constant_dynamic-slice_fusion.8, f32[16,128]{1,0:T(8,128)S(1)} %get-tuple-element.267, f32[16,128,640]{2,1,0:T(8,128)} %fusion.148), kind=kOutput, calls=%fused_computation.3.clone.1 | convolution fusion | flops 340789888 | bytes 16261120 | tf_op jit(solution)/shard_map/while/body/eval_jaxpr/hqk,qhv->khv/dot_general | solution.py:113
  506.8 9.0 fusion.150
  515.9 12.0 %bitcast_add_fusion.6 = f32[640,16,128]{0,2,1:T(8,128)} fusion(f32[640,16,128]{0,2,1:T(8,128)} %copy.90, bf16[128,16,128]{0,2,1:T(8,128)(2,1)S(1)} %constant_dynamic-slice_fusion.8, f32[16,128]{1,0:T(8,128)S(1)} %get-tuple-element.267, f32[16,128,640]{2,1,0:T(8,128)} %fusion.148), kind=kOutput, calls=%fused_computation.3.clone.1 | convolution fusion | flops 340789888 | bytes 16261120 | tf_op jit(solution)/shard_map/while/body/eval_jaxpr/hqk,qhv->khv/dot_general | solution.py:113
  605.0 8.9 fusion.150
  614.0 12.0 %bitcast_add_fusion.6 = f32[640,16,128]{0,2,1:T(8,128)} fusion(f32[640,16,128]{0,2,1:T(8,128)} %copy.90, bf16[128,16,128]{0,2,1:T(8,128)(2,1)S(1)} %constant_dynamic-slice_fusion.8, f32[16,128]{1,0:T(8,128)S(1)} %get-tuple-element.267, f32[16,128,640]{2,1,0:T(8,128)} %fusion.148), kind=kOutput, calls=%fused_computation.3.clone.1 | convolution fusion | flops 340789888 | bytes 16261120 | tf_op jit(solution)/shard_map/while/body/eval_jaxpr/hqk,qhv->khv/dot_general | solution.py:113
  703.1 8.9 fusion.150
  712.0 12.0 %bitcast_add_fusion.6 = f32[640,16,128]{0,2,1:T(8,128)} fusion(f32[640,16,128]{0,2,1:T(8,128)} %copy.90, bf16[128,16,128]{0,2,1:T(8,128)(2,1)S(1)} %constant_dynamic-slice_fusion.8, f32[16,128]{1,0:T(8,128)S(1)} %get-tuple-element.267, f32[16,128,640]{2,1,0:T(8,128)} %fusion.148), kind=kOutput, calls=%fused_computation.3.clone.1 | convolution fusion | flops 340789888 | bytes 16261120 | tf_op jit(solution)/shard_map/while/body/eval_jaxpr/hqk,qhv->khv/dot_general | solution.py:113
  801.2 9.0 fusion.150
  810.2 12.0 %bitcast_add_fusion.6 = f32[640,16,128]{0,2,1:T(8,128)} fusion(f32[640,16,128]{0,2,1:T(8,128)} %copy.90, bf16[128,16,128]{0,2,1:T(8,128)(2,1)S(1)} %constant_dynamic-slice_fusion.8, f32[16,128]{1,0:T(8,128)S(1)} %get-tuple-element.267, f32[16,128,640]{2,1,0:T(8,128)} %fusion.148), kind=kOutput, calls=%fused_computation.3.clone.1 | convolution fusion | flops 340789888 | bytes 16261120 | tf_op jit(solution)/shard_map/while/body/eval_jaxpr/hqk,qhv->khv/dot_general | solution.py:113
  868.2 9.7 %fusion.52 = f32[1024,512,1]{0,1,2:T(8,128)S(1)} fusion(bf16[16,512,128]{2,1,0:T(8,128)(2,1)S(1)} %copy-done, f32[1536,16,128]{2,0,1:T(8,128)} %get-tuple-element.79), kind=kOutput, calls=%fused_computation.58 | convolution fusion | flops 12884901888 | bytes 12582912 | tf_op jit(solution)/shard_map/thv,hdv->td/dot_general | solution.py:31
  890.0 8.3 collective-permute-done.1
  900.1 12.8 %copy.73 = bf16[8,128,16,192]{3,2,1,0:T(8,128)(2,1)} copy(bf16[8,128,16,192]{1,3,2,0:T(8,128)(2,1)} %get-tuple-element.77) | data formatting | bytes 12582912
  912.9 14.0 %reshape.100 = bf16[1024,3072]{1,0:T(8,128)(2,1)} reshape(bf16[8,128,16,192]{3,2,1,0:T(8,128)(2,1)} %copy.73) | data formatting | bytes 12582912
  926.9 35.8 %all-reduce.3.cloned.1.call-done = f32[1024,576]{0,1:T(8,128)} async-done(((f32[1024,576]{0,1:T(8,128)}), f32[1024,576]{0,1:T(8,128)}) %all-reduce.3.cloned.1.call-update) | async-done | bytes 2359312 | tf_op jit(solution)/shard_map/psum | solution.py:172
  (396 shorter events, 675.5 us)
Async XLA Ops:
  7.2 30.0 %copy-start = (bf16[16,512,128]{2,1,0:T(8,128)(2,1)S(1)}, bf16[16,512,128]{2,1,0:T(8,128)(2,1)}, u32[]{:S(2)}) copy-start(bf16[16,512,128]{2,1,0:T(8,128)(2,1)} %param.10) | copy-start | bytes 6291460
  7.2 955.5 %all-reduce.3.cloned.1.call-start = ((), (), s32[]{:S(2)}) async-start(), calls=%async_computation | async-start | bytes 4718592 | tf_op jit(solution)/shard_map/psum | solution.py:172
  9.3 22.9 %collective-permute-start = (bf16[512,576]{0,1:T(8,128)(2,1)}, bf16[512,576]{0,1:T(8,128)(2,1)}, u32[]{:S(2)}, u32[]{:S(2)}) collective-permute-start(bf16[512,576]{0,1:T(8,128)(2,1)} %slice.34), channel_id=1, source_target_pairs={{0,8},{8,16},{16,24},{1,9},{9,17},{17,25},{2,10},{10,18},{18,26},{... | collective-permute-start | bytes 1769480 | tf_op jit(solution)/shard_map/ppermute | solution.py:13
  16.7 17.6 %copy-start.7 = (bf16[1024,576]{1,0:T(8,128)(2,1)}, bf16[1024,576]{1,0:T(8,128)(2,1)S(1)}, u32[]{:S(2)}) copy-start(bf16[1024,576]{1,0:T(8,128)(2,1)S(1)} %copy.54) | copy-start | bytes 3538948
  76.5 46.3 %copy-start.4 = (bf16[128,16,128]{0,2,1:T(8,128)(2,1)}, bf16[128,16,128]{0,2,1:T(8,128)(2,1)S(1)}, u32[]{:S(2)}) copy-start(bf16[128,16,128]{0,2,1:T(8,128)(2,1)S(1)} %constant_dynamic-slice_fusion.8) | copy-start | bytes 1572868 | tf_op jit(solution)/shard_map/while
  134.8 12.5 %slice-start = ((s8[5242880]{0:T(1024)(128)(4,1)}), s8[1048576]{0:T(1024)(128)(4,1)S(1)}, s32[]{:S(2)}) async-start(s8[5242880]{0:T(1024)(128)(4,1)} %bitcast.114), calls=%async_computation.1 | async-start | bytes 2097152 | tf_op jit(solution)/shard_map/while
  174.7 46.4 %copy-start.4 = (bf16[128,16,128]{0,2,1:T(8,128)(2,1)}, bf16[128,16,128]{0,2,1:T(8,128)(2,1)S(1)}, u32[]{:S(2)}) copy-start(bf16[128,16,128]{0,2,1:T(8,128)(2,1)S(1)} %constant_dynamic-slice_fusion.8) | copy-start | bytes 1572868 | tf_op jit(solution)/shard_map/while
  233.0 12.5 %slice-start = ((s8[5242880]{0:T(1024)(128)(4,1)}), s8[1048576]{0:T(1024)(128)(4,1)S(1)}, s32[]{:S(2)}) async-start(s8[5242880]{0:T(1024)(128)(4,1)} %bitcast.114), calls=%async_computation.1 | async-start | bytes 2097152 | tf_op jit(solution)/shard_map/while
  272.9 46.4 %copy-start.4 = (bf16[128,16,128]{0,2,1:T(8,128)(2,1)}, bf16[128,16,128]{0,2,1:T(8,128)(2,1)S(1)}, u32[]{:S(2)}) copy-start(bf16[128,16,128]{0,2,1:T(8,128)(2,1)S(1)} %constant_dynamic-slice_fusion.8) | copy-start | bytes 1572868 | tf_op jit(solution)/shard_map/while
  331.2 12.5 %slice-start = ((s8[5242880]{0:T(1024)(128)(4,1)}), s8[1048576]{0:T(1024)(128)(4,1)S(1)}, s32[]{:S(2)}) async-start(s8[5242880]{0:T(1024)(128)(4,1)} %bitcast.114), calls=%async_computation.1 | async-start | bytes 2097152 | tf_op jit(solution)/shard_map/while
  371.3 46.4 %copy-start.4 = (bf16[128,16,128]{0,2,1:T(8,128)(2,1)}, bf16[128,16,128]{0,2,1:T(8,128)(2,1)S(1)}, u32[]{:S(2)}) copy-start(bf16[128,16,128]{0,2,1:T(8,128)(2,1)S(1)} %constant_dynamic-slice_fusion.8) | copy-start | bytes 1572868 | tf_op jit(solution)/shard_map/while
  429.6 12.5 %slice-start = ((s8[5242880]{0:T(1024)(128)(4,1)}), s8[1048576]{0:T(1024)(128)(4,1)S(1)}, s32[]{:S(2)}) async-start(s8[5242880]{0:T(1024)(128)(4,1)} %bitcast.114), calls=%async_computation.1 | async-start | bytes 2097152 | tf_op jit(solution)/shard_map/while
  469.5 46.4 %copy-start.4 = (bf16[128,16,128]{0,2,1:T(8,128)(2,1)}, bf16[128,16,128]{0,2,1:T(8,128)(2,1)S(1)}, u32[]{:S(2)}) copy-start(bf16[128,16,128]{0,2,1:T(8,128)(2,1)S(1)} %constant_dynamic-slice_fusion.8) | copy-start | bytes 1572868 | tf_op jit(solution)/shard_map/while
  527.8 12.5 %slice-start = ((s8[5242880]{0:T(1024)(128)(4,1)}), s8[1048576]{0:T(1024)(128)(4,1)S(1)}, s32[]{:S(2)}) async-start(s8[5242880]{0:T(1024)(128)(4,1)} %bitcast.114), calls=%async_computation.1 | async-start | bytes 2097152 | tf_op jit(solution)/shard_map/while
  567.7 46.3 %copy-start.4 = (bf16[128,16,128]{0,2,1:T(8,128)(2,1)}, bf16[128,16,128]{0,2,1:T(8,128)(2,1)S(1)}, u32[]{:S(2)}) copy-start(bf16[128,16,128]{0,2,1:T(8,128)(2,1)S(1)} %constant_dynamic-slice_fusion.8) | copy-start | bytes 1572868 | tf_op jit(solution)/shard_map/while
  626.0 12.5 %slice-start = ((s8[5242880]{0:T(1024)(128)(4,1)}), s8[1048576]{0:T(1024)(128)(4,1)S(1)}, s32[]{:S(2)}) async-start(s8[5242880]{0:T(1024)(128)(4,1)} %bitcast.114), calls=%async_computation.1 | async-start | bytes 2097152 | tf_op jit(solution)/shard_map/while
  665.8 46.3 %copy-start.4 = (bf16[128,16,128]{0,2,1:T(8,128)(2,1)}, bf16[128,16,128]{0,2,1:T(8,128)(2,1)S(1)}, u32[]{:S(2)}) copy-start(bf16[128,16,128]{0,2,1:T(8,128)(2,1)S(1)} %constant_dynamic-slice_fusion.8) | copy-start | bytes 1572868 | tf_op jit(solution)/shard_map/while
  724.0 12.5 %slice-start = ((s8[5242880]{0:T(1024)(128)(4,1)}), s8[1048576]{0:T(1024)(128)(4,1)S(1)}, s32[]{:S(2)}) async-start(s8[5242880]{0:T(1024)(128)(4,1)} %bitcast.114), calls=%async_computation.1 | async-start | bytes 2097152 | tf_op jit(solution)/shard_map/while
  763.9 46.4 %copy-start.4 = (bf16[128,16,128]{0,2,1:T(8,128)(2,1)}, bf16[128,16,128]{0,2,1:T(8,128)(2,1)S(1)}, u32[]{:S(2)}) copy-start(bf16[128,16,128]{0,2,1:T(8,128)(2,1)S(1)} %constant_dynamic-slice_fusion.8) | copy-start | bytes 1572868 | tf_op jit(solution)/shard_map/while
  861.5 16.4 %slice-start.4 = ((s8[12582912]{0:T(1024)(128)(4,1)}), s8[4194304]{0:T(1024)(128)(4,1)S(1)}, s32[]{:S(2)}) async-start(s8[12582912]{0:T(1024)(128)(4,1)} %bitcast.118), calls=%async_computation.5 | async-start | bytes 8388608
  861.5 16.4 %slice-start.5 = ((s8[12582912]{0:T(1024)(128)(4,1)}), s8[4194304]{0:T(1024)(128)(4,1)S(1)}, s32[]{:S(2)}) async-start(s8[12582912]{0:T(1024)(128)(4,1)} %bitcast.118), calls=%async_computation.6 | async-start | bytes 8388608
  868.2 14.9 %slice-start.7 = ((s8[12582912]{0:T(1024)(128)(4,1)}), s8[4194304]{0:T(1024)(128)(4,1)S(1)}, s32[]{:S(2)}) async-start(s8[12582912]{0:T(1024)(128)(4,1)} %bitcast.120), calls=%async_computation.8 | async-start | bytes 8388608
  868.2 14.9 %slice-start.8 = ((s8[12582912]{0:T(1024)(128)(4,1)}), s8[4194304]{0:T(1024)(128)(4,1)S(1)}, s32[]{:S(2)}) async-start(s8[12582912]{0:T(1024)(128)(4,1)} %bitcast.120), calls=%async_computation.9 | async-start | bytes 8388608
  881.6 16.7 %collective-permute-start.1 = (bf16[512,576]{0,1:T(8,128)(2,1)S(1)}, bf16[512,576]{0,1:T(8,128)(2,1)S(1)}, u32[]{:S(2)}, u32[]{:S(2)}) collective-permute-start(bf16[512,576]{0,1:T(8,128)(2,1)S(1)} %pad_maximum_fusion), channel_id=1, source_target_pairs={{8,0},{16,8},{24,16},{9,1},{17,9},{25,17},{10,2},{18,10},{26,18},{... | collective-permute-start | bytes 1769480 | tf_op jit(solution)/shard_map/ppermute | solution.py:13
  (71 other events, 426.2 us)
Sparse Core Ops, SparseCore 0:
  900.2 62.4 all-reduce.2
where the time goes:
time: 977 us; the launch traced here: 972 us
  matrix products  411 us (42%)
  local copies, waits for them, and re-layouts  405 us (41%)
  other arithmetic  71.5 us (7%)
  waiting for transfers between devices  44.1 us (5%)
  loops' own time  17.4 us (2%)
  between operations  14.7 us (2%)
    dot_general x8, matrix products, tile_advance(): jnp.einsum('hqk,qhv->khv', lowered_probabilities, g_block, preferred_elem...  95.6 us
    dynamic_slice x16, local copies, waits for them, and re-layouts, tile_advance(): lax.dynamic_slice_in_dim(acc_keys, first_row, span_rows, 0) + new_keys  89.9 us
    dynamic_slice x16, local copies, waits for them, and re-layouts, tile_advance(): lax.dynamic_slice_in_dim(acc_values, first_row, span_rows, 0) + new_values  89.6 us
    dynamic_update_slice x16, local copies, waits for them, and re-layouts, tile_advance(): lax.dynamic_update_slice_in_dim(acc_values, lax.dynamic_slice_in_dim(acc_...  85.6 us
    dot_general x8, matrix products, tile_advance(): jnp.einsum('hqk,khv->qhv', lowered_probabilities, v_block, preferred_elem...  72.1 us
    sub x8, other arithmetic, tile_advance(): expo = jnp.exp(logit_scores - peak)  57.9 us
    dynamic_update_slice x8, local copies, waits for them, and re-layouts, tile_advance(): lax.dynamic_update_slice_in_dim(acc_keys, lax.dynamic_slice_in_dim(acc_ke...  47.2 us
    unnamed x30, local copies, waits for them, and re-layouts  45.1 us
  transfers between devices with their start and end apart: 3, of which 2 were waited for; matrix products, arithmetic and copies ran while one was open for 5% of the time, Pallas kernels for 0%

commit v1 on v0

v1 whole, which is shorter than its diff:
```python
import functools
import math

import jax
import jax.numpy as jnp
from jax import lax
from jax.experimental import pallas as pl
from jax.experimental.pallas import tpu as pltpu
from jax.sharding import PartitionSpec as P

W = 512
T = 256
NEG = -1e30
NT = (((1,), (1,)), ((), ()))
NN = (((1,), (0,)), ((), ()))


def mm(a, b, dims=NN):
    return lax.dot_general(a, b, dims, preferred_element_type=jnp.float32)


def attend_kernel(
    prev_ref, own_ref, q_ref, uk_ref, uv_ref, g_ref, gq_ref, part_ref,
    kcat, kt, vs, pt, dst, acc, racc,
):
    step = pl.program_id(0)
    tokens = q_ref.shape[0]
    tiles = tokens // T
    reach = W // T
    chunks = tiles + reach
    dl = uk_ref.shape[1]
    scale = 192 ** -0.5
    c2 = scale * math.log2(math.e)
    first_bias = jnp.where(lax.axis_index("ctx") == 0, NEG, 0.0).astype(jnp.float32)

    @pl.when(step == 0)
    def _():
        acc[...] = jnp.zeros_like(acc)
        racc[...] = jnp.zeros_like(racc)

    wk = jnp.concatenate([uk_ref[0], uk_ref[1]], axis=1)
    wv = jnp.concatenate([uv_ref[0], uv_ref[1]], axis=1)
    wall = jnp.concatenate([wk, wv], axis=1)
    zero64 = jnp.zeros((T, 64), jnp.float32)
    zero128 = jnp.zeros((T, 128), jnp.float32)

    for j in range(chunks):
        rows = slice(j * T, (j + 1) * T)
        if j < reach:
            lat = prev_ref[j * T:(j + 1) * T, :]
        else:
            lat = own_ref[(j - reach) * T:(j - reach + 1) * T, :]
        kr = lat[:, dl:].astype(jnp.float32)
        k2 = mm(lat[:, :dl], wk)
        v2 = mm(lat[:, :dl], wv)
        ka = jnp.concatenate([k2[:, :128], kr, zero64], axis=1).astype(jnp.bfloat16)
        kb = pltpu.roll(jnp.concatenate([k2[:, 128:], kr, zero64], axis=1), 64, 1).astype(jnp.bfloat16)
        kcat[0, rows, :] = ka
        kcat[1, rows, :] = kb
        kt[0, :, rows] = ka.T
        kt[1, :, rows] = kb.T
        vs[rows, :] = v2.astype(jnp.bfloat16)

    u = lax.broadcasted_iota(jnp.int32, (T, T), 0)
    r = lax.broadcasted_iota(jnp.int32, (T, T), 1)
    low_keep = u > r
    lane = lax.broadcasted_iota(jnp.int32, (T, 128), 1)

    def tile(t, e):
        qrows = slice(t * T, (t + 1) * T)
        q = q_ref[qrows, e * 128:e * 128 + 256]
        g = g_ref[qrows, e * 128:e * 128 + 128]
        ss = []
        for a in range(reach + 1):
            rows = slice((t + a) * T, (t + a + 1) * T)
            s = mm(kcat[e, rows, :], q, NT)
            if a == 0:
                s = jnp.where(low_keep, s, NEG)
            if a == reach:
                s = jnp.where(low_keep, NEG, s)
            if t + a < reach:
                s = s + first_bias
            ss.append(s)
        peak = jnp.max(ss[0], axis=0, keepdims=True)
        for s in ss[1:]:
            peak = jnp.maximum(peak, jnp.max(s, axis=0, keepdims=True))
        es = [jnp.exp2((s - peak) * c2) for s in ss]
        total = sum(jnp.sum(x, axis=0, keepdims=True) for x in es)
        inv = 1.0 / total
        ds_list = []
        dps = []
        delta = jnp.zeros((1, T), jnp.float32)
        for a in range(reach + 1):
            rows = slice((t + a) * T, (t + a + 1) * T)
            dp = mm(vs[rows, e * 128:e * 128 + 128], g, NT)
            dps.append(dp)
            delta = delta + jnp.sum(es[a] * dp, axis=0, keepdims=True)
        delta = delta * inv
        dq = jnp.zeros((256, T), jnp.float32)
        for a in range(reach + 1):
            rows = slice((t + a) * T, (t + a + 1) * T)
            p = es[a] * inv
            pt[e, rows, qrows] = p.astype(jnp.bfloat16)
            ds = (p * (dps[a] - delta)).astype(jnp.bfloat16)
            dst[e, rows, qrows] = ds
            ds_list.append(ds)
        dq = mm(kt[e, :, t * T:(t + reach + 1) * T], jnp.concatenate(ds_list, axis=0))
        return (dq * scale).T

    def chunk(j):
        rows = slice(j * T, (j + 1) * T)
        t0, t1 = max(0, j - reach), min(tiles - 1, j)
        qrows = slice(t0 * T, (t1 + 1) * T)
        dka = mm(dst[0, rows, qrows], q_ref[qrows, 0:256]) * scale
        dkb = mm(dst[1, rows, qrows], q_ref[qrows, 128:384]) * scale
        dva = mm(pt[0, rows, qrows], g_ref[qrows, 0:128])
        dvb = mm(pt[1, rows, qrows], g_ref[qrows, 128:256])
        racc[rows, :] += jnp.where(lane < 64, dka[:, 128:], dkb[:, 128:])
        dkb = pltpu.roll(dkb, 192, 1)[:, :128]
        grads = jnp.concatenate(
            [dka[:, :128], dkb, dva, dvb], axis=1
        ).astype(jnp.bfloat16)
        acc[rows, :] += mm(grads, wall, NT)

    for t in range(tiles):
        qrows = slice(t * T, (t + 1) * T)
        a = tile(t, 0)
        b = tile(t, 1)
        gq_ref[qrows, 0:128] = a[:, :128].astype(jnp.bfloat16)
        gq_ref[qrows, 128:256] = (a[:, 128:] + b[:, :128]).astype(jnp.bfloat16)
        gq_ref[qrows, 256:384] = b[:, 128:].astype(jnp.bfloat16)
        chunk(t)
    for j in range(tiles, chunks):
        chunk(j)

    @pl.when(step == pl.num_programs(0) - 1)
    def _():
        part_ref[:, :dl] = acc[...].astype(part_ref.dtype)
        part_ref[:, dl:] = (racc[:, :64] + racc[:, 64:]).astype(part_ref.dtype)


def attend(previous, latent_kv, queries, w_uk, w_uv, grad_out):
    tokens = queries.shape[0]
    heads = w_uk.shape[0]
    dl = w_uk.shape[1]
    rows = tokens + W
    width = latent_kv.shape[1]
    full = lambda s: pl.BlockSpec(s, lambda i: (0,) * len(s))
    return pl.pallas_call(
        attend_kernel,
        grid=(heads // 2,),
        in_specs=[
            full(previous.shape),
            full(latent_kv.shape),
            pl.BlockSpec((tokens, 384), lambda i: (0, i)),
            pl.BlockSpec((2, dl, 128), lambda i: (i, 0, 0)),
            pl.BlockSpec((2, dl, 128), lambda i: (i, 0, 0)),
            pl.BlockSpec((tokens, 256), lambda i: (0, i)),
        ],
        out_specs=[
            pl.BlockSpec((tokens, 384), lambda i: (0, i)),
            full((rows, width)),
        ],
        out_shape=[
            jax.ShapeDtypeStruct(queries.shape, jnp.bfloat16),
            jax.ShapeDtypeStruct((rows, width), jnp.float32),
        ],
        scratch_shapes=[
            pltpu.VMEM((2, rows, 256), jnp.bfloat16),
            pltpu.VMEM((2, 256, rows), jnp.bfloat16),
            pltpu.VMEM((rows, 256), jnp.bfloat16),
            pltpu.VMEM((2, rows, tokens), jnp.bfloat16),
            pltpu.VMEM((2, rows, tokens), jnp.bfloat16),
            pltpu.VMEM((rows, dl), jnp.float32),
            pltpu.VMEM((rows, 128), jnp.float32),
        ],
        compiler_params=pltpu.CompilerParams(vmem_limit_bytes=56 * 2 ** 20),
    )(previous, latent_kv, queries, w_uk, w_uv, grad_out)


def shift(array, axis, by):
    peers = lax.axis_size(axis)
    return lax.ppermute(array, axis, [(i, i + by) for i in range(peers) if 0 <= i + by < peers])


def shards(queries, latent_kv, w_uk, w_uv, grad_out):
    tokens = queries.shape[0]
    previous = shift(latent_kv[tokens - W:], "ctx", 1)
    grad_queries, part = attend(previous, latent_kv, queries, w_uk, w_uv, grad_out)
    returned = shift(part[:W].astype(jnp.bfloat16), "ctx", -1).astype(jnp.float32)
    extra = jnp.concatenate(
        [jnp.zeros((tokens - W, part.shape[1]), jnp.float32), returned], axis=0
    )
    grad_latent = lax.psum_scatter(part[W:] + extra, "head", scatter_dimension=0, tiled=True)
    return grad_queries, grad_latent


def solution(mesh):
    in_specs = (
        P("ctx", "head"),
        P("ctx", None),
        P("head", None, None),
        P("head", None, None),
        P("ctx", "head"),
    )
    out_specs = (P("ctx", "head"), P(("ctx", "head"), None))
    return jax.shard_map(shards, mesh=mesh, in_specs=in_specs, out_specs=out_specs, check_vma=False)
```

time: 977 us -> 176 us (0.18)
  matrix products: 411 us -> 0 us
  local copies, waits for them, and re-layouts: 405 us -> 8.39 us
  Pallas kernels: 0 us -> 73.8 us
  other arithmetic: 71.5 us -> 3.46 us
  waiting for transfers between devices: 44.1 us -> 69.9 us
  loops' own time: 17.4 us -> 0 us
    dot_general x78 -> x0, matrix products: 411 us -> none  [the longest x8 95.6 us: tile_advance(): jnp.einsum('hqk,qhv->khv', lowered_probabilities, g_block, preferred_elem...]
    dynamic_slice x57 -> x0, local copies, waits for them, and re-layouts: 197 us -> none  [the longest x16 89.9 us: tile_advance(): lax.dynamic_slice_in_dim(acc_keys, first_row, span_rows, 0) + new_keys]
    dynamic_update_slice x24 -> x0, local copies, waits for them, and re-layouts: 133 us -> none  [the longest x16 85.6 us: tile_advance(): lax.dynamic_update_slice_in_dim(acc_values, lax.dynamic_slice_in_dim(acc_...]
    pallas_call x0 -> x1, Pallas kernels: none -> 73.8 us  [attend(): pl.pallas_call(attend_kernel, grid=(heads // 2,), in_specs=[full(previous...]
    sub x8 -> x0, other arithmetic: 57.9 us -> none  [tile_advance(): expo = jnp.exp(logit_scores - peak)]
    reduce_scatter x0 -> x1, waiting for transfers between devices: none -> 44.2 us  [shards(): lax.psum_scatter(part[W:] + extra, 'head', scatter_dimension=0, tiled=True)]
    unnamed x30 -> x2, local copies, waits for them, and re-layouts: 45.1 us -> 4.26 us
    psum x1 -> x0, waiting for transfers between devices: 35.8 us -> none  [shards(): lax.psum(project_back(own_keys, own_values, own_rope, key_weight, value_w...]
  transfers between devices with their start and end apart: 3 -> 3, of which waited for: 2 -> 3; matrix products, arithmetic and copies ran while one was open for 5% -> 1% of each run, Pallas kernels for 0% -> 0%
where the time goes in v1:
time: 176 us
  Pallas kernels  73.8 us (42%)
  waiting for transfers between devices  69.9 us (40%)
  between operations  14.1 us (8%)
  local copies, waits for them, and re-layouts  8.39 us (5%)
  starting transfers between devices  6.29 us (4%)
  other arithmetic  3.46 us (2%)
    pallas_call x1, Pallas kernels, attend(): pl.pallas_call(attend_kernel, grid=(heads // 2,), in_specs=[full(previous...  73.8 us
    reduce_scatter x1, waiting for transfers between devices, shards(): lax.psum_scatter(part[W:] + extra, 'head', scatter_dimension=0, tiled=True)  44.2 us
    ppermute x2, waiting for transfers between devices, shift(): lax.ppermute(array, axis, [(i, i + by) for i in range(peers) if 0 <= i +...  25.6 us
    ppermute x2, starting transfers between devices, shift(): lax.ppermute(array, axis, [(i, i + by) for i in range(peers) if 0 <= i +...  6.26 us
    unnamed x2, local copies, waits for them, and re-layouts  4.26 us
  transfers between devices with their start and end apart: 3, of which 3 were waited for; matrix products, arithmetic and copies ran while one was open for 1% of the time, Pallas kernels for 0%

profile of v1, /device:TPU:0, one launch (start us, length us, event | category | flops | bytes accessed | tf_op | source)
XLA Modules:
  0.0 175.9 jit_solution(803934511850206949)
XLA Ops:
  7.2 0.0 reduce-scatter.2.cloned.1.call-start
  7.2 1.1 slice.10
  8.3 5.0 %collective-permute-start = (bf16[512,576]{0,1:T(8,128)(2,1)S(1)}, bf16[512,576]{0,1:T(8,128)(2,1)S(1)}, u32[]{:S(2)}, u32[]{:S(2)}) collective-permute-start(bf16[512,576]{0,1:T(8,128)(2,1)S(1)} %slice.10), channel_id=1, source_target_pairs={{0,8},{8,16},{16,24},{1,9},{9,17},{17,25},{2,10},{10,18},{18,26},{... | collective-permute-start | bytes 1769480 | tf_op jit(solution)/shard_map/ppermute | solution.py:183
  13.3 2.4 %copy.11.own_ref = bf16[1024,576]{1,0:T(8,128)(2,1)} copy(bf16[1024,576]{0,1:T(8,128)(2,1)} %param.6) | data formatting | bytes 2359296 | tf_op args[1]
  15.7 10.1 %collective-permute-done = bf16[512,576]{0,1:T(8,128)(2,1)S(1)} collective-permute-done((bf16[512,576]{0,1:T(8,128)(2,1)S(1)}, bf16[512,576]{0,1:T(8,128)(2,1)S(1)}, u32[]{:S(2)}, u32[]{:S(2)}) %collective-permute-start) | collective-permute-done | bytes 589856 | tf_op jit(solution)/shard_map/ppermute | solution.py:183
  25.8 1.1 copy.10.prev_ref
  26.9 73.8 %shard_map.68 = (bf16[1024,3072]{1,0:T(8,128)(2,1)}, f32[1536,576]{1,0:T(8,128)}) custom-call(bf16[512,576]{1,0:T(8,128)(2,1)} %copy.10.prev_ref, bf16[1024,576]{1,0:T(8,128)(2,1)} %copy.11.own_ref, bf16[1024,3072]{1,0:T(8,128)(2,1)} %q_ref.1, bf16[16,512,128]{2,1,0:T(8,128)(2,1)} %uk_ref.1, bf16[16,512,128]{2,1,0:T(8,128)(2,1)} %uv_ref.1, ...), custom_call_target="tpu_custom_call" | custom-call | tf_op jit(solution)/shard_map/pallas_call | solution.py:149
  100.8 1.4 slice.16
  102.2 0.2 copy.12
  102.4 1.3 collective-permute-start.1
  103.7 15.5 %collective-permute-done.1 = bf16[512,576]{0,1:T(8,128)(2,1)S(1)} collective-permute-done((bf16[512,576]{0,1:T(8,128)(2,1)S(1)}, bf16[512,576]{0,1:T(8,128)(2,1)S(1)}, u32[]{:S(2)}, u32[]{:S(2)}) %collective-permute-start.1) | collective-permute-done | bytes 589856 | tf_op jit(solution)/shard_map/ppermute | solution.py:183
  119.2 0.3 copy.13
  119.5 3.5 %convert_add_fusion = f32[1024,576]{1,0:T(8,128)} fusion(f32[1536,576]{1,0:T(8,128)} %get-tuple-element.5, bf16[512,576]{1,0:T(8,128)(2,1)S(1)} %copy.13), kind=kLoop, calls=%fused_computation | loop fusion | flops 1179648 | bytes 5308416 | tf_op jit(solution)/shard_map/add | solution.py:194
  123.0 0.0 reduce-scatter.2.cloned.1.call-update
  123.0 44.2 %reduce-scatter.2.cloned.1.call-done = f32[128,576]{1,0:T(8,128)} async-done(((f32[1024,576]{1,0:T(8,128)}), f32[128,576]{1,0:T(8,128)}) %reduce-scatter.2.cloned.1.call-update) | async-done | bytes 294928 | tf_op jit(solution)/shard_map/reduce_scatter | solution.py:194
  167.2 1.8 %copy.14 = f32[128,576]{0,1:T(8,128)} copy(f32[128,576]{1,0:T(8,128)} %reduce-scatter.2.cloned.1.call-done) | data formatting | bytes 589824
Async XLA Ops:
  7.2 160.1 %reduce-scatter.2.cloned.1.call-start = ((), (), s32[]{:S(2)}) async-start(), calls=%async_computation.1 | async-start | bytes 2949120 | tf_op jit(solution)/shard_map/reduce_scatter | solution.py:194
  8.3 17.5 %collective-permute-start = (bf16[512,576]{0,1:T(8,128)(2,1)S(1)}, bf16[512,576]{0,1:T(8,128)(2,1)S(1)}, u32[]{:S(2)}, u32[]{:S(2)}) collective-permute-start(bf16[512,576]{0,1:T(8,128)(2,1)S(1)} %slice.10), channel_id=1, source_target_pairs={{0,8},{8,16},{16,24},{1,9},{9,17},{17,25},{2,10},{10,18},{18,26},{... | collective-permute-start | bytes 1769480 | tf_op jit(solution)/shard_map/ppermute | solution.py:183
  102.4 16.8 %collective-permute-start.1 = (bf16[512,576]{0,1:T(8,128)(2,1)S(1)}, bf16[512,576]{0,1:T(8,128)(2,1)S(1)}, u32[]{:S(2)}, u32[]{:S(2)}) collective-permute-start(bf16[512,576]{0,1:T(8,128)(2,1)S(1)} %copy.12), channel_id=1, source_target_pairs={{8,0},{16,8},{24,16},{9,1},{17,9},{25,17},{10,2},{18,10},{26,18},{... | collective-permute-start | bytes 1769480 | tf_op jit(solution)/shard_map/ppermute | solution.py:183
Sparse Core Ops, SparseCore 0:
  123.1 44.0 reduce-scatter.1

commit v2 on v1

--- a/solution.py
+++ b/solution.py
@@ -21,7 +21,7 @@
 
 def attend_kernel(
     prev_ref, own_ref, q_ref, uk_ref, uv_ref, g_ref, gq_ref, part_ref,
-    kcat, kt, vs, pt, dst, acc, racc,
+    kcat, kt, vs, pt, dst, acc, racc, lats,
 ):
     step = pl.program_id(0)
     tokens = q_ref.shape[0]
@@ -37,6 +37,9 @@
     def _():
         acc[...] = jnp.zeros_like(acc)
         racc[...] = jnp.zeros_like(racc)
+        for j in range(chunks):
+            ref, i = (prev_ref, j) if j < reach else (own_ref, j - reach)
+            lats[j * T:(j + 1) * T, :] = ref[:, i * T:(i + 1) * T].T
 
     wk = jnp.concatenate([uk_ref[0], uk_ref[1]], axis=1)
     wv = jnp.concatenate([uv_ref[0], uv_ref[1]], axis=1)
@@ -46,10 +49,7 @@
 
     for j in range(chunks):
         rows = slice(j * T, (j + 1) * T)
-        if j < reach:
-            lat = prev_ref[j * T:(j + 1) * T, :]
-        else:
-            lat = own_ref[(j - reach) * T:(j - reach + 1) * T, :]
+        lat = lats[rows, :]
         kr = lat[:, dl:].astype(jnp.float32)
         k2 = mm(lat[:, :dl], wk)
         v2 = mm(lat[:, :dl], wv)
@@ -144,7 +144,7 @@
     heads = w_uk.shape[0]
     dl = w_uk.shape[1]
     rows = tokens + W
-    width = latent_kv.shape[1]
+    width = latent_kv.shape[0]
     full = lambda s: pl.BlockSpec(s, lambda i: (0,) * len(s))
     return pl.pallas_call(
         attend_kernel,
@@ -163,7 +163,7 @@
         ],
         out_shape=[
             jax.ShapeDtypeStruct(queries.shape, jnp.bfloat16),
-            jax.ShapeDtypeStruct((rows, width), jnp.float32),
+            jax.ShapeDtypeStruct((rows, width), jnp.bfloat16),
         ],
         scratch_shapes=[
             pltpu.VMEM((2, rows, 256), jnp.bfloat16),
@@ -173,6 +173,7 @@
             pltpu.VMEM((2, rows, tokens), jnp.bfloat16),
             pltpu.VMEM((rows, dl), jnp.float32),
             pltpu.VMEM((rows, 128), jnp.float32),
+            pltpu.VMEM((rows, width), jnp.bfloat16),
         ],
         compiler_params=pltpu.CompilerParams(vmem_limit_bytes=56 * 2 ** 20),
     )(previous, latent_kv, queries, w_uk, w_uv, grad_out)
@@ -183,16 +184,164 @@
     return lax.ppermute(array, axis, [(i, i + by) for i in range(peers) if 0 <= i + by < peers])
 
 
+MESH = pl.DeviceIdType.MESH
+
+
+def reduce_kernel(
+    part_ref, final_ref, out_ref, r1, r1e, r2, r2e, s2, s2e, eout, ein,
+    ss1, rs1, ss1e, rs1e, ss2, rs2, ss2e, rs2e, sse, rse, ctxs=1, heads=2,
+):
+    c = lax.axis_index("ctx")
+    h = lax.axis_index("head")
+    m0, core = h // 2, h % 2
+    half = heads // 2
+    blk = out_ref.shape[0]
+    tokens = blk * heads
+    er = W // heads
+    per = blk // er
+    sib = m0 * 2 + 1 - core
+    away = tokens - W + h * er
+    dest = away // blk
+    slot = (away % blk) // er
+    takes = jnp.logical_and(h * blk >= tokens - W, c < ctxs - 1)
+    gives = c > 0
+    giver = jnp.maximum((h * blk - (tokens - W)) // er, 0)
+    below = jnp.maximum(c - 1, 0)
+    above = jnp.minimum(c + 1, ctxs - 1)
+
+    barrier = pltpu.get_barrier_semaphore()
+
+    def greet(cc, hh):
+        pl.semaphore_signal(barrier, inc=1, device_id=(cc, hh), device_id_type=MESH)
+
+    greet(c, sib)
+    for k in range(half - 1):
+        greet(c, ((m0 + 1 + k) % half) * 2 + core)
+
+    @pl.when(gives)
+    def _():
+        greet(below, dest)
+
+    @pl.when(takes)
+    def _():
+        for i in range(per):
+            greet(above, giver + i)
+
+    pl.semaphore_wait(
+        barrier, half + gives.astype(jnp.int32) + per * takes.astype(jnp.int32)
+    )
+
+    def rows_of(m, parity, size, base):
+        return pl.ds(pl.multiple_of(base + (2 * m + parity) * size, 16), size)
+
+    def remote(src, dst, send, recv, cc, hh):
+        return pltpu.make_async_remote_copy(
+            src_ref=src, dst_ref=dst, send_sem=send, recv_sem=recv,
+            device_id=(cc, hh), device_id_type=MESH,
+        )
+
+    first = {}
+    for name, size, base, land, sends, recvs in (
+        ("e", er, 0, r1e, ss1e, rs1e), ("o", blk, W, r1, ss1, rs1),
+    ):
+        for k in range(half):
+            m = (m0 + 1 + k) % half
+            cp = remote(
+                part_ref.at[rows_of(m, 1 - core, size, base)], land.at[k],
+                sends.at[k], recvs.at[k], c, sib,
+            )
+            cp.start()
+            first[name, k] = cp
+
+    second = {}
+    kept = {}
+    for name, size, base, land, out, land2, sends, recvs in (
+        ("e", er, 0, r1e, s2e, r2e, ss2e, rs2e), ("o", blk, W, r1, s2, r2, ss2, rs2),
+    ):
+        for k in range(half):
+            m = (m0 + 1 + k) % half
+            first[name, k].wait_recv()
+            both = part_ref[rows_of(m, core, size, base), :].astype(jnp.float32)
+            both = both + land[k].astype(jnp.float32)
+            if k == half - 1:
+                if name == "e":
+                    eout[...] = both
+                else:
+                    out_ref[...] = both
+            else:
+                out[k] = both.astype(jnp.bfloat16)
+                cp = remote(out.at[k], land2.at[k], sends.at[k], recvs.at[k], c, 2 * m + core)
+                cp.start()
+                second[name, k] = cp
+
+    for k in range(half - 1):
+        second["e", k].wait_recv()
+    edge = eout[...]
+    for k in range(half - 1):
+        edge = edge + r2e[k].astype(jnp.float32)
+    s2e[half - 1] = edge.astype(jnp.bfloat16)
+
+    @pl.when(gives)
+    def _():
+        remote(s2e.at[half - 1], ein.at[slot], sse, rse.at[slot], below, dest).start()
+
+    total = out_ref[...]
+    for k in range(half - 1):
+        second["o", k].wait_recv()
+        total = total + r2[k].astype(jnp.float32)
+    out_ref[...] = total
+
+    @pl.when(takes)
+    def _():
+        for i in range(per):
+            remote(s2e.at[half - 1], ein.at[i], sse, rse.at[i], above, h).wait_recv()
+            out_ref[i * er:(i + 1) * er, :] += ein[i].astype(jnp.float32)
+
+    final_ref[...] = out_ref[...].T
+
+    for cp in first.values():
+        cp.wait_send()
+    for cp in second.values():
+        cp.wait_send()
+
+    @pl.when(gives)
+    def _():
+        remote(s2e.at[half - 1], ein.at[slot], sse, rse.at[slot], below, dest).wait_send()
+
+
+def reduce_part(part, tokens):
+    ctxs, heads = lax.axis_size("ctx"), lax.axis_size("head")
+    width = part.shape[1]
+    half, blk, er = heads // 2, tokens // heads, W // heads
+    dma = pltpu.SemaphoreType.DMA
+    vm = lambda n, rows: pltpu.VMEM((n, rows, width), jnp.bfloat16)
+    return pl.pallas_call(
+        functools.partial(reduce_kernel, ctxs=ctxs, heads=heads),
+        out_shape=jax.ShapeDtypeStruct((width, blk), jnp.float32),
+        in_specs=[pl.BlockSpec(memory_space=pltpu.VMEM)],
+        out_specs=pl.BlockSpec(memory_space=pltpu.VMEM),
+        scratch_shapes=[
+            pltpu.VMEM((blk, width), jnp.float32),
+            vm(half, blk), vm(half, er), vm(half, blk), vm(half, er),
+            vm(half, blk), vm(half, er),
+            pltpu.VMEM((er, width), jnp.float32),
+            vm(blk // er, er),
+            dma((half,)), dma((half,)), dma((half,)), dma((half,)),
+            dma((half,)), dma((half,)), dma((half,)), dma((half,)),
+            dma, dma((blk // er,)),
+        ],
+        compiler_params=pltpu.CompilerParams(
+            collective_id=0, has_side_effects=True, vmem_limit_bytes=32 * 2 ** 20
+        ),
+    )(part)
+
+
 def shards(queries, latent_kv, w_uk, w_uv, grad_out):
     tokens = queries.shape[0]
-    previous = shift(latent_kv[tokens - W:], "ctx", 1)
-    grad_queries, part = attend(previous, latent_kv, queries, w_uk, w_uv, grad_out)
-    returned = shift(part[:W].astype(jnp.bfloat16), "ctx", -1).astype(jnp.float32)
-    extra = jnp.concatenate(
-        [jnp.zeros((tokens - W, part.shape[1]), jnp.float32), returned], axis=0
-    )
-    grad_latent = lax.psum_scatter(part[W:] + extra, "head", scatter_dimension=0, tiled=True)
-    return grad_queries, grad_latent
+    latent_t = latent_kv.T
+    previous = shift(latent_t[:, tokens - W:], "ctx", 1)
+    grad_queries, part = attend(previous, latent_t, queries, w_uk, w_uv, grad_out)
+    return grad_queries, reduce_part(part, tokens).T
 
 
 def solution(mesh):

time: 176 us -> 115 us (0.65)
  waiting for transfers between devices: 69.9 us -> 12.5 us
  Pallas kernels: 73.8 us -> 91.7 us
  between operations: 14.1 us -> 0.65 us
  local copies, waits for them, and re-layouts: 8.39 us -> 4.19 us
  other arithmetic: 3.46 us -> 0 us
    reduce_scatter x1 -> x0, waiting for transfers between devices: 44.2 us -> none  [shards(): lax.psum_scatter(part[W:] + extra, 'head', scatter_dimension=0, tiled=True)]
    pallas_call x0 -> x1, Pallas kernels: none -> 17.8 us  [reduce_part(): pl.pallas_call(functools.partial(reduce_kernel, ctxs=ctxs, heads=heads),...]
    ppermute x2 -> x1, waiting for transfers between devices: 25.6 us -> 12.5 us  [shift(): lax.ppermute(array, axis, [(i, i + by) for i in range(peers) if 0 <= i +...]
    add x1 -> x0, other arithmetic: 3.46 us -> none  [shards(): part[W:] + extra]
    ppermute x2 -> x1, starting transfers between devices: 6.26 us -> 4.96 us  [shift(): lax.ppermute(array, axis, [(i, i + by) for i in range(peers) if 0 <= i +...]
    unnamed x2 -> x5, local copies, waits for them, and re-layouts: 4.26 us -> 3.08 us
  transfers between devices with their start and end apart: 3 -> 1, of which waited for: 3 -> 1; matrix products, arithmetic and copies ran while one was open for 1% -> 0% of each run, Pallas kernels for 0% -> 0%
where the time goes in v2:
time: 115 us; the launch traced here: 114 us
  Pallas kernels  91.7 us (80%)
  waiting for transfers between devices  12.5 us (11%)
  starting transfers between devices  4.96 us (4%)
  local copies, waits for them, and re-layouts  4.19 us (4%)
    pallas_call x1, Pallas kernels, attend(): pl.pallas_call(attend_kernel, grid=(heads // 2,), in_specs=[full(previous...  73.8 us
    pallas_call x1, Pallas kernels, reduce_part(): pl.pallas_call(functools.partial(reduce_kernel, ctxs=ctxs, heads=heads),...  17.8 us
    ppermute x1, waiting for transfers between devices, shift(): lax.ppermute(array, axis, [(i, i + by) for i in range(peers) if 0 <= i +...  12.5 us
    ppermute x1, starting transfers between devices, shift(): lax.ppermute(array, axis, [(i, i + by) for i in range(peers) if 0 <= i +...  4.96 us
    unnamed x5, local copies, waits for them, and re-layouts  3.08 us
  transfers between devices with their start and end apart: 1, of which 1 were waited for; matrix products, arithmetic and copies ran while one was open for 0% of the time, Pallas kernels for 0%

profile of v2, /device:TPU:0, one launch (start us, length us, event | category | flops | bytes accessed | tf_op | source)
XLA Modules:
  0.0 114.0 jit_solution(14955433312651871993)
XLA Ops:
  0.6 1.1 slice.4
  1.7 5.0 %collective-permute-start = (bf16[576,512]{1,0:T(8,128)(2,1)S(1)}, bf16[576,512]{1,0:T(8,128)(2,1)S(1)}, u32[]{:S(2)}, u32[]{:S(2)}) collective-permute-start(bf16[576,512]{1,0:T(8,128)(2,1)S(1)} %slice.4), channel_id=1, source_target_pairs={{0,8},{8,16},{16,24},{1,9},{9,17},{17,25},{2,10},{10,18},{18,26},{... | collective-permute-start | bytes 1769480 | tf_op jit(solution)/shard_map/ppermute | solution.py:184
  6.7 12.5 %collective-permute-done.prev_ref = bf16[576,512]{1,0:T(8,128)(2,1)S(1)} collective-permute-done((bf16[576,512]{1,0:T(8,128)(2,1)S(1)}, bf16[576,512]{1,0:T(8,128)(2,1)S(1)}, u32[]{:S(2)}, u32[]{:S(2)}) %collective-permute-start) | collective-permute-done | bytes 589856 | tf_op jit(solution)/shard_map/ppermute | solution.py:184
  19.2 0.0 copy-start.1
  19.2 0.8 copy-done.1
  20.1 73.8 %shard_map.68 = (bf16[1024,3072]{1,0:T(8,128)(2,1)}, bf16[1536,576]{1,0:T(8,128)(2,1)}) custom-call(bf16[576,512]{1,0:T(8,128)(2,1)} %copy-done.1, bf16[576,1024]{1,0:T(8,128)(2,1)} %bitcast.4, bf16[1024,3072]{1,0:T(8,128)(2,1)} %q_ref.1, bf16[16,512,128]{2,1,0:T(8,128)(2,1)} %uk_ref.1, bf16[16,512,128]{2,1,0:T(8,128)(2,1)} %uv_ref.1, bf16[1024,2048]{1,0:T(8,128)(2,1)} %g_ref.1), custom_call_target="tpu_custom_call" | custom-call | tf_op jit(solution)/shard_map/pallas_call | solution.py:149
  93.9 0.0 copy-start
  93.9 1.5 %copy-done = bf16[1536,576]{1,0:T(8,128)(2,1)S(1)} copy-done((bf16[1536,576]{1,0:T(8,128)(2,1)S(1)}, bf16[1536,576]{1,0:T(8,128)(2,1)}, u32[]{:S(2)}) %copy-start) | copy-done | bytes 1769496
  95.5 17.8 %shard_map.69 = f32[576,128]{1,0:T(8,128)S(1)} custom-call(bf16[1536,576]{1,0:T(8,128)(2,1)S(1)} %copy-done), custom_call_target="tpu_custom_call" | custom-call | tf_op jit(solution)/shard_map/pallas_call | solution.py:318
  113.3 0.7 copy.8
Async XLA Ops:
  1.7 17.5 %collective-permute-start = (bf16[576,512]{1,0:T(8,128)(2,1)S(1)}, bf16[576,512]{1,0:T(8,128)(2,1)S(1)}, u32[]{:S(2)}, u32[]{:S(2)}) collective-permute-start(bf16[576,512]{1,0:T(8,128)(2,1)S(1)} %slice.4), channel_id=1, source_target_pairs={{0,8},{8,16},{16,24},{1,9},{9,17},{17,25},{2,10},{10,18},{18,26},{... | collective-permute-start | bytes 1769480 | tf_op jit(solution)/shard_map/ppermute | solution.py:184
  19.2 0.8 copy-start.1
  93.9 1.5 %copy-start = (bf16[1536,576]{1,0:T(8,128)(2,1)S(1)}, bf16[1536,576]{1,0:T(8,128)(2,1)}, u32[]{:S(2)}) copy-start(bf16[1536,576]{1,0:T(8,128)(2,1)} %get-tuple-element.5.part_ref) | copy-start | bytes 5308420

commit v3 on v2

--- a/solution.py
+++ b/solution.py
@@ -19,10 +19,12 @@
     return lax.dot_general(a, b, dims, preferred_element_type=jnp.float32)
 
 
-def attend_kernel(
-    prev_ref, own_ref, q_ref, uk_ref, uv_ref, g_ref, gq_ref, part_ref,
-    kcat, kt, vs, pt, dst, acc, racc, lats,
-):
+def attend_kernel(*refs, behind):
+    prev_ref, own_ref, q_ref, uk_ref, uv_ref, g_ref = refs[:6]
+    if behind:
+        later_ref = refs[6]
+        refs = refs[2:]
+    gq_ref, part_ref, kcat, kt, vs, pt, dst, acc, racc, lats = refs[6:]
     step = pl.program_id(0)
     tokens = q_ref.shape[0]
     tiles = tokens // T
@@ -78,7 +80,7 @@
                 s = jnp.where(low_keep, s, NEG)
             if a == reach:
                 s = jnp.where(low_keep, NEG, s)
-            if t + a < reach:
+            if behind and t + a < reach:
                 s = s + first_bias
             ss.append(s)
         peak = jnp.max(ss[0], axis=0, keepdims=True)
@@ -135,36 +137,57 @@
 
     @pl.when(step == pl.num_programs(0) - 1)
     def _():
-        part_ref[:, :dl] = acc[...].astype(part_ref.dtype)
-        part_ref[:, dl:] = (racc[:, :64] + racc[:, 64:]).astype(part_ref.dtype)
-
-
-def attend(previous, latent_kv, queries, w_uk, w_uv, grad_out):
-    tokens = queries.shape[0]
+        rope = racc[:, :64] + racc[:, 64:]
+        if not behind:
+            part_ref[:, :dl] = acc[...].astype(part_ref.dtype)
+            part_ref[:, dl:] = rope.astype(part_ref.dtype)
+        else:
+            part_ref[:W, :dl] = acc[:W, :].astype(part_ref.dtype)
+            part_ref[:W, dl:] = rope[:W].astype(part_ref.dtype)
+            later = later_ref[:W, :].astype(jnp.float32)
+            part_ref[W:2 * W, :dl] = (acc[W:, :] + later[:, :dl]).astype(part_ref.dtype)
+            part_ref[W:2 * W, dl:] = (rope[W:] + later[:, dl:]).astype(part_ref.dtype)
+            part_ref[2 * W:, :] = later_ref[W:, :]
+
+
+def attend(previous, latent_t, queries, w_uk, w_uv, grad_out, later=None, grads=None):
+    behind = later is not None
+    tokens = W
+    place = 0 if behind else 1
     heads = w_uk.shape[0]
     dl = w_uk.shape[1]
     rows = tokens + W
-    width = latent_kv.shape[0]
+    width = latent_t.shape[0]
     full = lambda s: pl.BlockSpec(s, lambda i: (0,) * len(s))
+    in_specs = [
+        full((width, W)),
+        pl.BlockSpec((width, tokens), lambda i: (0, place)),
+        pl.BlockSpec((tokens, 384), lambda i: (place, i)),
+        pl.BlockSpec((2, dl, 128), lambda i: (i, 0, 0)),
+        pl.BlockSpec((2, dl, 128), lambda i: (i, 0, 0)),
+        pl.BlockSpec((tokens, 256), lambda i: (place, i)),
+    ]
+    operands = [previous, latent_t, queries, w_uk, w_uv, grad_out]
+    if behind:
+        in_specs += [full(later.shape), pl.BlockSpec(memory_space=pl.ANY)]
+        operands += [later, grads]
+    part_rows = rows + W if behind else rows
     return pl.pallas_call(
-        attend_kernel,
+        functools.partial(attend_kernel, behind=behind),
         grid=(heads // 2,),
-        in_specs=[
-            full(previous.shape),
-            full(latent_kv.shape),
-            pl.BlockSpec((tokens, 384), lambda i: (0, i)),
-            pl.BlockSpec((2, dl, 128), lambda i: (i, 0, 0)),
-            pl.BlockSpec((2, dl, 128), lambda i: (i, 0, 0)),
-            pl.BlockSpec((tokens, 256), lambda i: (0, i)),
-        ],
+        in_specs=in_specs,
         out_specs=[
-            pl.BlockSpec((tokens, 384), lambda i: (0, i)),
-            full((rows, width)),
+            pl.BlockSpec((tokens, 384), lambda i: (place, i)),
+            full((part_rows, width)),
         ],
         out_shape=[
             jax.ShapeDtypeStruct(queries.shape, jnp.bfloat16),
-            jax.ShapeDtypeStruct((rows, width), jnp.bfloat16),
+            jax.ShapeDtypeStruct((part_rows, width), jnp.bfloat16),
         ],
+        input_output_aliases={7: 0} if behind else {},
+        cost_estimate=pl.CostEstimate(
+            flops=heads * 2 * 10 ** 9, bytes_accessed=16 * 10 ** 6, transcendentals=0
+        ),
         scratch_shapes=[
             pltpu.VMEM((2, rows, 256), jnp.bfloat16),
             pltpu.VMEM((2, 256, rows), jnp.bfloat16),
@@ -176,7 +199,7 @@
             pltpu.VMEM((rows, width), jnp.bfloat16),
         ],
         compiler_params=pltpu.CompilerParams(vmem_limit_bytes=56 * 2 ** 20),
-    )(previous, latent_kv, queries, w_uk, w_uv, grad_out)
+    )(*operands)
 
 
 def shift(array, axis, by):
@@ -340,7 +363,10 @@
     tokens = queries.shape[0]
     latent_t = latent_kv.T
     previous = shift(latent_t[:, tokens - W:], "ctx", 1)
-    grad_queries, part = attend(previous, latent_t, queries, w_uk, w_uv, grad_out)
+    grads, later = attend(latent_t, latent_t, queries, w_uk, w_uv, grad_out)
+    grad_queries, part = attend(
+        previous, latent_t, queries, w_uk, w_uv, grad_out, later, grads
+    )
     return grad_queries, reduce_part(part, tokens).T
 
 

time: 115 us -> 112 us (0.974)
  waiting for transfers between devices: 12.5 us -> 0.01 us
  Pallas kernels: 91.7 us -> 102 us
    ppermute x1, waiting for transfers between devices: 12.5 us -> 0.01 us  [shift(): lax.ppermute(array, axis, [(i, i + by) for i in range(peers) if 0 <= i +...]
    pallas_call x1 -> x2, Pallas kernels: 73.8 us -> 84.1 us  [attend(): pl.pallas_call(functools.partial(attend_kernel, behind=behind), grid=(hea...]
  transfers between devices with their start and end apart: 1 -> 1, of which waited for: 1 -> 0; matrix products, arithmetic and copies ran while one was open for 0% -> 0% of each run, Pallas kernels for 0% -> 37%
where the time goes in v3:
time: 112 us
  Pallas kernels  102 us (91%)
  starting transfers between devices  4.96 us (4%)
  local copies, waits for them, and re-layouts  4.18 us (4%)
    pallas_call x2, Pallas kernels, attend(): pl.pallas_call(functools.partial(attend_kernel, behind=behind), grid=(hea...  84.1 us
    pallas_call x1, Pallas kernels, reduce_part(): pl.pallas_call(functools.partial(reduce_kernel, ctxs=ctxs, heads=heads),...  17.9 us
    ppermute x1, starting transfers between devices, shift(): lax.ppermute(array, axis, [(i, i + by) for i in range(peers) if 0 <= i +...  4.96 us
    unnamed x5, local copies, waits for them, and re-layouts  3.07 us
  transfers between devices with their start and end apart: 1, of which 0 were waited for; matrix products, arithmetic and copies ran while one was open for 0% of the time, Pallas kernels for 37%

profile of v3, /device:TPU:0, one launch (start us, length us, event | category | flops | bytes accessed | tf_op | source)
XLA Modules:
  0.0 111.8 jit_solution(16506221496764928496)
XLA Ops:
  0.6 1.1 slice.4
  1.7 5.0 %collective-permute-start = (bf16[576,512]{1,0:T(8,128)(2,1)S(1)}, bf16[576,512]{1,0:T(8,128)(2,1)S(1)}, u32[]{:S(2)}, u32[]{:S(2)}) collective-permute-start(bf16[576,512]{1,0:T(8,128)(2,1)S(1)} %slice.4), channel_id=1, source_target_pairs={{0,8},{8,16},{16,24},{1,9},{9,17},{17,25},{2,10},{10,18},{18,26},{... | collective-permute-start | bytes 1769480 | tf_op jit(solution)/shard_map/ppermute | solution.py:207
  6.7 41.7 %shard_map.68 = (bf16[1024,3072]{1,0:T(8,128)(2,1)}, bf16[1024,576]{1,0:T(8,128)(2,1)}) custom-call(bf16[576,1024]{1,0:T(8,128)(2,1)} %bitcast.4, bf16[576,1024]{1,0:T(8,128)(2,1)} %bitcast.5, bf16[1024,3072]{1,0:T(8,128)(2,1)} %refs_2_.3, bf16[16,512,128]{2,1,0:T(8,128)(2,1)} %refs_3_.3, bf16[16,512,128]{2,1,0:T(8,128)(2,1)} %refs_4_.3, ...), custom_call_target="tpu_custom_call" | custom-call | flops 32000000000 | bytes 16000000 | tf_op jit(solution)/shard_map/pallas_call | solution.py:175
  48.4 0.0 collective-permute-done.refs_0_
  48.4 0.0 copy-start.1
  48.4 0.8 copy-done.1
  49.2 42.4 %shard_map.69 = (bf16[1024,3072]{1,0:T(8,128)(2,1)}, bf16[1536,576]{1,0:T(8,128)(2,1)}) custom-call(bf16[576,512]{1,0:T(8,128)(2,1)} %copy-done.1, bf16[576,1024]{1,0:T(8,128)(2,1)} %bitcast.6, bf16[1024,3072]{1,0:T(8,128)(2,1)} %refs_2_.3, bf16[16,512,128]{2,1,0:T(8,128)(2,1)} %refs_3_.3, ...), custom_call_target="tpu_custom_call", output_to_operand_aliasing={{0}: (7, {})} | custom-call | flops 32000000000 | bytes 16000000 | tf_op jit(solution)/shard_map/pallas_call | solution.py:175
  91.6 0.0 copy-start
  91.6 1.5 %copy-done = bf16[1536,576]{1,0:T(8,128)(2,1)S(1)} copy-done((bf16[1536,576]{1,0:T(8,128)(2,1)S(1)}, bf16[1536,576]{1,0:T(8,128)(2,1)}, u32[]{:S(2)}) %copy-start) | copy-done | bytes 1769496
  93.1 17.9 %shard_map.70 = f32[576,128]{1,0:T(8,128)S(1)} custom-call(bf16[1536,576]{1,0:T(8,128)(2,1)S(1)} %copy-done), custom_call_target="tpu_custom_call" | custom-call | tf_op jit(solution)/shard_map/pallas_call | solution.py:341
  111.1 0.7 copy.10
Async XLA Ops:
  1.7 46.7 %collective-permute-start = (bf16[576,512]{1,0:T(8,128)(2,1)S(1)}, bf16[576,512]{1,0:T(8,128)(2,1)S(1)}, u32[]{:S(2)}, u32[]{:S(2)}) collective-permute-start(bf16[576,512]{1,0:T(8,128)(2,1)S(1)} %slice.4), channel_id=1, source_target_pairs={{0,8},{8,16},{16,24},{1,9},{9,17},{17,25},{2,10},{10,18},{18,26},{... | collective-permute-start | bytes 1769480 | tf_op jit(solution)/shard_map/ppermute | solution.py:207
  48.4 0.8 copy-start.1
  91.6 1.5 %copy-start = (bf16[1536,576]{1,0:T(8,128)(2,1)S(1)}, bf16[1536,576]{1,0:T(8,128)(2,1)}, u32[]{:S(2)}) copy-start(bf16[1536,576]{1,0:T(8,128)(2,1)} %get-tuple-element.9.part_ref) | copy-start | bytes 5308420
